TPU v7x, 512 devices: a whole 4x8x8 slice. The times are simulated.
512 devices in a mesh: row: 32 (over y, x), col: 16 (over z, core).
Axes of the slice: x: 4, y: 8, z: 8, core: 2. Of those that a mesh axis runs over, the one named last changes fastest.
Arguments:
- diag_tiles: float32 [32, 256, 256], P('row'), as said below
- left_fac: bfloat16 [32, 32, 256, 128], P('row', 'col'), as said below
- right_fac: bfloat16 [32, 32, 256, 128], P('row', 'col'), as said below
- ranks: int32 [32, 32], replicated, may hold values from 16 to 128, as said below
Outputs:
- factored: float32 [32, 32, 256, 256], P('row', 'col')
Inputs may be any that keep to these rules, and one draw needn't show every extreme that they name: `ranks`: every entry is a multiple of 16; in every draw some tile below the diagonal has rank 128, and the mean rank is about a third of 128. `diag_tiles`: every tile is symmetric; the first diagonal tile and the updated second diagonal tile M are positive definite. `left_fac`: entries have mean zero and deviation one. `right_fac`: entries have mean zero and deviation one over the square root of 128.
All inputs are finite; a program needn't handle non-finite values.
Results may differ from a plain program's by a relative error of at most 0.0003.
Values sent between devices are 32-bit elements; how exact they have to be, the bound alone decides.
A program may use at most 64 MiB of HBM per device.

v0:
```python
import jax
import jax.numpy as jnp
from jax import lax
from jax.sharding import PartitionSpec as P

PRECISE = lax.Precision.HIGHEST


def from_root(shard, axis, root):
    mine = lax.axis_index(axis) == root
    return lax.psum(jnp.where(mine, shard, jnp.zeros_like(shard)), axis)


def lower_solve(factor, stacked):
    pieces, tile_width, rank_cap = stacked.shape
    flattened = jnp.transpose(stacked, (1, 0, 2)).reshape(tile_width, pieces * rank_cap)
    solved = lax.linalg.triangular_solve(factor, flattened, left_side=True, lower=True)
    return jnp.transpose(solved.reshape(tile_width, pieces, rank_cap), (1, 0, 2))


def expand(left_basis, weights):
    return jnp.einsum("nbr,ncr->nbc", left_basis, weights, precision=PRECISE)


def correction(head_basis, row_solved, pivot_solved):
    mixing = jnp.einsum("nbr,bs->nrs", row_solved, pivot_solved, precision=PRECISE)
    return -jnp.einsum("bs,nrs->nbr", head_basis, mixing, precision=PRECISE)


def take_slot(stacked, holder_slot):
    return lax.dynamic_index_in_dim(stacked, holder_slot, 0, keepdims=False)


def shards(diag_tiles, left_fac, right_fac, ranks):
    grid_rows = lax.axis_size("row")
    grid_cols = lax.axis_size("col")
    row_here = lax.axis_index("row")
    col_here = lax.axis_index("col")
    row_slots, col_slots, tile_width, rank_cap = left_fac.shape
    tile_rows = jnp.arange(row_slots, dtype=jnp.int32) * grid_rows + row_here
    tile_cols = jnp.arange(col_slots, dtype=jnp.int32) * grid_cols + col_here
    local_ranks = jnp.take(jnp.take(ranks, tile_rows, axis=0), tile_cols, axis=1)
    columns_live = jnp.arange(rank_cap, dtype=jnp.int32)[None, None, :] < local_ranks[:, :, None]
    left_bases = jnp.where(columns_live[:, :, None, :], left_fac.astype(jnp.float32), 0.0)
    right_coefs = right_fac.astype(jnp.float32)
    first_pivot = from_root(jnp.linalg.cholesky(diag_tiles[0]), "row", 0)
    first_local = lower_solve(first_pivot, right_coefs[:, 0])
    first_row_basis, first_row_solved = (
        from_root(left_bases[:, 0], "col", 0),
        from_root(first_local, "col", 0),
    )
    gathered_basis = []
    gathered_solved = []
    for column_slot in range(col_slots):
        tile_number = column_slot * grid_cols + col_here
        holder_slot = tile_number // grid_rows
        received = (
            from_root(take_slot(first_row_basis, holder_slot), "row", tile_number % grid_rows),
            from_root(take_slot(first_row_solved, holder_slot), "row", tile_number % grid_rows),
        )
        gathered_basis.append(received[0])
        gathered_solved.append(received[1])
    first_col_basis = jnp.stack(gathered_basis)
    first_col_solved = jnp.stack(gathered_solved)
    pivot_basis = first_row_basis[0]
    pivot_solved = first_row_solved[0]
    pivot_cross = jnp.einsum("br,bs->rs", pivot_solved, pivot_solved, precision=PRECISE)
    partial_term = jnp.matmul(pivot_basis, pivot_cross, precision=PRECISE)
    shifted = diag_tiles[0] - jnp.matmul(partial_term, pivot_basis.T, precision=PRECISE)
    second_pivot = from_root(jnp.linalg.cholesky(shifted), "row", 1)
    second_local = lower_solve(second_pivot, right_coefs[:, 0])
    first_row_dense = expand(first_row_basis, first_row_solved)
    first_col_dense = expand(first_col_basis, first_col_solved)
    pieces_dense = []
    local_head = lax.linalg.triangular_solve(
        second_pivot, first_col_basis[0], left_side=True, lower=True
    )
    local_minus = correction(local_head, first_row_solved, first_col_solved[0])
    second_row = (
        from_root(left_bases[:, 0], "col", 1),
        from_root(second_local, "col", 1),
        from_root(local_minus, "col", 1),
    )
    second_row_dense = expand(second_row[0], second_row[1]) + expand(first_row_basis, second_row[2])
    for column_slot in range(col_slots):
        tile_number = column_slot * grid_cols + col_here
        holder_slot = tile_number // grid_rows
        received = (
            from_root(take_slot(second_row[0], holder_slot), "row", tile_number % grid_rows),
            from_root(take_slot(second_row[1], holder_slot), "row", tile_number % grid_rows),
            from_root(take_slot(second_row[2], holder_slot), "row", tile_number % grid_rows),
        )
        own_dense = expand(received[0][None], received[1][None]) + expand(
            first_col_basis[column_slot][None], received[2][None]
        )
        pieces_dense.append(own_dense[0])
    second_col_dense = jnp.stack(pieces_dense)
    dense_front = jnp.einsum("lmbr,lmcr->lmbc", left_bases, right_coefs, precision=PRECISE)
    updates = jnp.einsum("lbk,mck->lmbc", first_row_dense, first_col_dense, precision=PRECISE)
    updates = updates + jnp.einsum(
        "lbk,mck->lmbc", second_row_dense, second_col_dense, precision=PRECISE
    )
    schur = dense_front - updates
    row_ids = tile_rows[:, None, None, None]
    col_ids = tile_cols[None, :, None, None]
    chosen = jnp.where(
        col_ids == 0,
        first_row_dense[:, None],
        jnp.where(col_ids == 1, second_row_dense[:, None], schur),
    )
    return jnp.where(col_ids < row_ids, chosen, 0.0)


def solution(mesh):
    in_specs = (P("row", None, None), P("row", "col", None, None), P("row", "col", None, None), P())
    out_specs = P("row", "col", None, None)
    return jax.shard_map(shards, mesh=mesh, in_specs=in_specs, out_specs=out_specs, check_vma=False)
```

profile of v0, /device:TPU:64, one launch (start us, length us, event | category | flops | bytes accessed | tf_op | source)
XLA Modules:
  0.0 864.5 jit_solution(8564235674343520192)
XLA Ops:
  6.5 1.1 copy.12
  7.8 11.7 %cholesky.130 = f32[128,128]{1,0:T(8,128)S(1)} custom-call(f32[128,128]{1,0:T(8,128)S(1)} %cholesky.194), custom_call_target="Cholesky" | custom-call | tf_op jit(solution)/shard_map/jit(cholesky)/cholesky | solution.py:46
  19.5 9.8 %custom-call.14 = f32[1,128,128]{1,2,0:T(8,128)S(1)} custom-call(f32[1,128,128]{2,1,0:T(8,128)S(1)} %get-tuple-element.96), custom_call_target="InvertDiagBlocksLowerTriangular" | custom-call | tf_op jit(solution)/shard_map/jit(cholesky)/cholesky | solution.py:46
  29.8 11.7 %cholesky.147 = f32[128,128]{1,0:T(8,128)S(1)} custom-call(f32[128,128]{1,0:T(8,128)S(1)} %convolution_subtract_fusion.5), custom_call_target="Cholesky" | custom-call | tf_op jit(solution)/shard_map/jit(cholesky)/cholesky | solution.py:46
  41.6 0.7 compare_reduce_fusion.2
  43.6 0.7 fusion.28
  44.6 0.6 copy-done.10
  45.3 0.7 fusion.51
  46.0 0.6 gather_fusion
  46.9 0.7 select_bitcast_fusion.1
  47.6 155.9 %all-reduce.11.cloned.1.call-done = f32[256,256]{1,0:T(8,128)} async-done(((f32[256,256]{1,0:T(8,128)}), f32[256,256]{1,0:T(8,128)}) %all-reduce.11.cloned.1.call-update) | async-done | bytes 262160 | tf_op jit(solution)/shard_map/psum | solution.py:11
  203.5 1.0 fusion.27
  204.6 4.1 while.7
  204.6 0.6 fusion.102
  205.2 1.4 bitcast_dynamic-update-slice_fusion.4
  206.7 0.6 fusion.102
  207.3 1.4 bitcast_dynamic-update-slice_fusion.4
  208.7 19.7 %custom-call.15 = f32[2,128,128]{1,2,0:T(8,128)S(1)} custom-call(f32[2,128,128]{2,1,0:T(8,128)S(1)} %get-tuple-element.38), custom_call_target="InvertDiagBlocksLowerTriangular" | custom-call | tf_op jit(solution)/shard_map/triangular_solve/custom-call.0 | solution.py:17
  229.2 0.7 maximum_select_fusion
  229.9 109.7 %all-reduce.19.cloned.1.call-done = (f32[256,128]{1,0:T(8,128)}, f32[256,128]{1,0:T(8,128)}) async-done(((f32[256,128]{1,0:T(8,128)}, f32[256,128]{1,0:T(8,128)}), (f32[256,128]{1,0:T(8,128)}, f32[256,128]{1,0:T(8,128)})) %all-reduce.19.cloned.1.call-update) | async-done | bytes 262160 | tf_op jit(solution)/shard_map/psum | solution.py:11
  339.6 1.4 fusion.60
  341.1 0.8 broadcast_select_fusion.8
  342.0 0.8 broadcast_select_fusion.7
  343.7 11.7 %cholesky.164 = f32[128,128]{1,0:T(8,128)S(1)} custom-call(f32[128,128]{1,0:T(8,128)S(1)} %cholesky.197), custom_call_target="Cholesky" | custom-call | tf_op jit(solution)/shard_map/jit(cholesky)/cholesky | solution.py:70
  355.4 9.8 %custom-call.16 = f32[1,128,128]{1,2,0:T(8,128)S(1)} custom-call(f32[1,128,128]{2,1,0:T(8,128)S(1)} %get-tuple-element.92), custom_call_target="InvertDiagBlocksLowerTriangular" | custom-call | tf_op jit(solution)/shard_map/jit(cholesky)/cholesky | solution.py:70
  365.7 11.7 %cholesky.181 = f32[128,128]{1,0:T(8,128)S(1)} custom-call(f32[128,128]{1,0:T(8,128)S(1)} %convolution_subtract_fusion.3), custom_call_target="Cholesky" | custom-call | tf_op jit(solution)/shard_map/jit(cholesky)/cholesky | solution.py:70
  377.5 0.7 compare_reduce_fusion
  378.2 0.6 compare_reduce_fusion.1
  380.2 0.7 select_select_fusion
  381.2 161.0 %all-reduce.15.cloned.1.call-done = (f32[256,128]{1,0:T(8,128)}, f32[256,128]{1,0:T(8,128)}, f32[256,256]{1,0:T(8,128)}) async-done(((f32[256,128]{1,0:T(8,128)}, f32[256,128]{1,0:T(8,128)}, f32[256,256]{1,0:T(8,128)}), (f32[256,128]{1,0:T(8,128)}, f32[256,128]{1,0:T(8,128)}, f32[256,256]{1,0:T(8,128)})) %all-reduce.15.cloned.1.call-update) | async-done | bytes 524304 | tf_op jit(solution)/shard_map/psum | solution.py:11
  542.2 1.0 fusion.25
  543.2 4.1 while.8
  543.8 1.4 bitcast_dynamic-update-slice_fusion.5
  545.2 0.6 fusion.103
  545.8 1.4 bitcast_dynamic-update-slice_fusion.5
  547.3 19.7 %custom-call.17 = f32[2,128,128]{1,2,0:T(8,128)S(1)} custom-call(f32[2,128,128]{2,1,0:T(8,128)S(1)} %get-tuple-element.39), custom_call_target="InvertDiagBlocksLowerTriangular" | custom-call | tf_op jit(solution)/shard_map/triangular_solve/custom-call.0 | solution.py:17
  568.1 0.6 copy-done.8
  569.6 0.7 maximum_select_fusion.1
  570.2 0.9 fusion.8
  571.2 110.5 %all-reduce.17.cloned.1.call-done = (f32[256,128]{1,0:T(8,128)}, f32[256,128]{1,0:T(8,128)}, f32[256,128]{1,0:T(8,128)}) async-done(((f32[256,128]{1,0:T(8,128)}, f32[256,128]{1,0:T(8,128)}, f32[256,128]{1,0:T(8,128)}), (f32[256,128]{1,0:T(8,128)}, f32[256,128]{1,0:T(8,128)}, f32[256,128]{1,0:T(8,128)})) %all-reduce.17.cloned.1.call-update) | async-done | bytes 393232 | tf_op jit(solution)/shard_map/psum | solution.py:11
  681.8 1.7 broadcast_select_fusion.3
  683.4 0.7 broadcast_select_fusion.4
  684.4 0.7 broadcast_select_fusion.5
  686.9 163.7 %all-reduce.13.cloned.1.call-done = (f32[256,128]{1,0:T(8,128)}, f32[1,256,128]{2,1,0:T(8,128)}, f32[256,128]{1,0:T(8,128)}, f32[256,128]{1,0:T(8,128)}, f32[256...) async-done(((f32[256,128]{1,0:T(8,128)}, f32[1,256,128]{2,1,0:T(8,128)}, f32[256,128]{1,0:T(8,128)}, f32[256,128]{1,0:T(8,128)}, ...) | async-done | bytes 1048592 | tf_op jit(solution)/shard_map/psum | solution.py:11
  850.6 1.4 fusion.64
  855.4 0.6 fusion.21
  856.1 0.6 fusion
  856.7 1.2 fusion.4
  (91 shorter events, 11.9 us)
Async XLA Ops:
  6.5 197.0 %all-reduce.11.cloned.1.call-start = ((), (), s32[]{:S(2)}) async-start(), calls=%async_computation | async-start | bytes 524288 | tf_op jit(solution)/shard_map/psum | solution.py:11
  6.5 1.2 copy-start.3
  44.3 0.9 copy-start.10
  44.3 295.3 %all-reduce.19.cloned.1.call-start = ((), (), s32[]{:S(2)}) async-start(), calls=%async_computation.4 | async-start | bytes 524288 | tf_op jit(solution)/shard_map/psum | solution.py:11
  46.0 0.9 copy-start.4
  229.9 312.3 %all-reduce.15.cloned.1.call-start = ((), (), s32[]{:S(2)}) async-start(), calls=%async_computation.2 | async-start | bytes 1048576 | tf_op jit(solution)/shard_map/psum | solution.py:11
  339.6 1.4 copy-start
  341.1 1.0 copy-start.1
  380.9 300.9 %all-reduce.17.cloned.1.call-start = ((), (), s32[]{:S(2)}) async-start(), calls=%async_computation.3 | async-start | bytes 786432 | tf_op jit(solution)/shard_map/psum | solution.py:11
  547.3 20.0 %copy-start.2 = (f32[256,128]{1,0:T(8,128)S(1)}, f32[256,128]{1,0:T(8,128)}, u32[]{:S(2)}) copy-start(f32[256,128]{1,0:T(8,128)} %get-tuple-element.65) | copy-start | bytes 393220
  567.8 0.9 copy-start.8
  571.2 279.4 %all-reduce.13.cloned.1.call-start = ((), (), s32[]{:S(2)}) async-start(), calls=%async_computation.1 | async-start | bytes 2097152 | tf_op jit(solution)/shard_map/psum | solution.py:11
  681.8 1.7 copy-start.7
  683.4 1.0 copy-start.6
  685.6 0.9 copy-start.5
  850.6 1.4 copy-start.14
  852.0 0.9 copy-start.12
  852.0 1.0 copy-start.13
  852.9 0.9 copy-start.9
  852.9 1.0 copy-start.11
  853.9 0.9 copy-start.15
Sparse Core Ops, SparseCore 0:
  44.5 159.0 all-reduce.10
  230.0 109.6 all-reduce.18
  381.0 161.0 all-reduce.14
  571.3 110.4 all-reduce.16
  686.6 163.9 all-reduce.12
where the time goes:
time: 865 us; the launch traced here: 864 us
  waiting for transfers between devices  701 us (81%)
  other arithmetic  119 us (14%)
  between operations  16.3 us (2%)
  local copies, waits for them, and re-layouts  14.2 us (2%)
  matrix products  13.4 us (2%)
    psum x5, waiting for transfers between devices, from_root(): return lax.psum(jnp.where(mine, shard, jnp.zeros_like(shard)), axis)  701 us
    another operation x5, other arithmetic, lower_solve(): lax.linalg.triangular_solve(factor, flattened, left_side=True, lower=True)  41.3 us
    another operation x7, other arithmetic, shards(): second_pivot = from_root(jnp.linalg.cholesky(shifted), 'row', 1)  34.7 us
    another operation x6, other arithmetic, shards(): first_pivot = from_root(jnp.linalg.cholesky(diag_tiles[0]), 'row', 0)  34 us
  transfers between devices with their start and end apart: 5, of which 5 were waited for; matrix products, arithmetic and copies ran while one was open for 0% of the time, Pallas kernels for 0%

commit v1 on v0

--- a/solution.py
+++ b/solution.py
@@ -6,9 +6,15 @@
 PRECISE = lax.Precision.HIGHEST
 
 
+def summed_here(shard, axis):
+    parts = lax.all_gather(shard, axis, axis=0, tiled=False)
+    result = parts.sum(axis=0)
+    return result
+
+
 def from_root(shard, axis, root):
     mine = lax.axis_index(axis) == root
-    return lax.psum(jnp.where(mine, shard, jnp.zeros_like(shard)), axis)
+    return summed_here(jnp.where(mine, shard, jnp.zeros_like(shard)), axis)
 
 
 def lower_solve(factor, stacked):

time: 865 us -> 1410 us (1.63)
  the two profiles are of different devices: /device:TPU:64 before, /device:TPU:8 now
where the time goes in v1:
time: 1410 us; the launch traced here: 1400 us
  waiting for transfers between devices  1200 us (85%)
  other arithmetic  158 us (11%)
  between operations  16.7 us (1%)
    all_gather x17, waiting for transfers between devices, summed_here(): parts = lax.all_gather(shard, axis, axis=0, tiled=False)  1200 us
    another operation x5, other arithmetic, lower_solve(): lax.linalg.triangular_solve(factor, flattened, left_side=True, lower=True)  39.4 us
    reduce_sum x16, other arithmetic, summed_here(): result = parts.sum(axis=0)  38.6 us
    another operation x7, other arithmetic, shards(): second_pivot = from_root(jnp.linalg.cholesky(shifted), 'row', 1)  34.7 us
    another operation x6, other arithmetic, shards(): first_pivot = from_root(jnp.linalg.cholesky(diag_tiles[0]), 'row', 0)  34 us
  transfers between devices with their start and end apart: 17, of which 17 were waited for; matrix products, arithmetic and copies ran while one was open for 7% of the time, Pallas kernels for 0%

profile of v1, /device:TPU:8, one launch (start us, length us, event | category | flops | bytes accessed | tf_op | source)
XLA Modules:
  0.0 1401.2 jit_solution(2309819090814478668)
XLA Ops:
  8.7 11.7 cholesky.130
  20.4 9.8 custom-call.14
  30.7 11.7 cholesky.147
  49.1 103.1 %all-gather.37.cloned.1.call-done = f32[8192,256]{1,0:T(8,128)} async-done(((f32[256,256]{1,0:T(8,128)}), f32[8192,256]{1,0:T(8,128)}) %all-gather.37.cloned.1.call-update) | async-done | bytes 8388624 | tf_op jit(solution)/shard_map/all_gather | solution.py:10
  152.1 3.9 reduce_sum.154
  156.2 4.0 while.7
  156.8 1.4 bitcast_dynamic-update-slice_fusion.4
  158.8 1.4 bitcast_dynamic-update-slice_fusion.4
  160.1 19.7 %custom-call.15 = f32[2,128,128]{1,2,0:T(8,128)S(1)} custom-call(f32[2,128,128]{2,1,0:T(8,128)S(1)} %get-tuple-element.38), custom_call_target="InvertDiagBlocksLowerTriangular" | custom-call | tf_op jit(solution)/shard_map/triangular_solve/custom-call.0 | solution.py:23
  181.4 15.2 %all-gather.33.cloned.1.call-done = f32[16,1,256,128]{3,2,1,0:T(8,128)} async-done(((f32[1,1,256,128]{3,2,1,0:T(8,128)}), f32[16,1,256,128]{3,2,1,0:T(8,128)}) %all-gather.33.cloned.1.call-update) | async-done | bytes 2097168 | tf_op jit(solution)/shard_map/all_gather | solution.py:10
  196.5 1.7 reduce_sum.153
  198.2 41.5 %all-gather.39.cloned.1.call-done = f32[4096,128]{1,0:T(8,128)} async-done(((f32[256,128]{1,0:T(8,128)}), f32[4096,128]{1,0:T(8,128)}) %all-gather.39.cloned.1.call-update) | async-done | bytes 2097168 | tf_op jit(solution)/shard_map/all_gather | solution.py:10
  239.8 1.7 reduce.13
  242.7 11.7 cholesky.164
  254.5 9.8 custom-call.16
  264.8 11.7 cholesky.181
  282.5 97.8 %all-gather.41.cloned.1.call-done = f32[8192,256]{1,0:T(8,128)} async-done(((f32[256,256]{1,0:T(8,128)}), f32[8192,256]{1,0:T(8,128)}) %all-gather.41.cloned.1.call-update) | async-done | bytes 8388624 | tf_op jit(solution)/shard_map/all_gather | solution.py:10
  380.3 3.9 reduce_sum.157
  384.3 4.1 while.8
  384.9 1.4 bitcast_dynamic-update-slice_fusion.5
  387.0 1.4 bitcast_dynamic-update-slice_fusion.5
  388.4 19.7 %custom-call.17 = f32[2,128,128]{1,2,0:T(8,128)S(1)} custom-call(f32[2,128,128]{2,1,0:T(8,128)S(1)} %get-tuple-element.39), custom_call_target="InvertDiagBlocksLowerTriangular" | custom-call | tf_op jit(solution)/shard_map/triangular_solve/custom-call.0 | solution.py:23
  409.6 60.1 %all-gather.47.cloned.1.call-done = f32[8192,128]{1,0:T(8,128)} async-done(((f32[256,128]{1,0:T(8,128)}), f32[8192,128]{1,0:T(8,128)}) %all-gather.47.cloned.1.call-update) | async-done | bytes 4194320 | tf_op jit(solution)/shard_map/all_gather | solution.py:10
  469.8 2.4 reduce_sum.160
  472.2 85.3 %all-gather.45.cloned.1.call-done = f32[8192,128]{1,0:T(8,128)} async-done(((f32[256,128]{1,0:T(8,128)}), f32[8192,128]{1,0:T(8,128)}) %all-gather.45.cloned.1.call-update) | async-done | bytes 4194320 | tf_op jit(solution)/shard_map/all_gather | solution.py:10
  557.4 2.4 reduce_sum.159
  562.1 38.0 %all-gather.35.cloned.1.call-done = f32[16,1,256,128]{3,2,1,0:T(8,128)} async-done(((f32[1,1,256,128]{3,2,1,0:T(8,128)}), f32[16,1,256,128]{3,2,1,0:T(8,128)}) %all-gather.35.cloned.1.call-update) | async-done | bytes 2097168 | tf_op jit(solution)/shard_map/all_gather | solution.py:10
  600.1 1.7 reduce_sum.156
  604.6 38.9 %all-gather.43.cloned.1.call-done = f32[4096,128]{1,0:T(8,128)} async-done(((f32[256,128]{1,0:T(8,128)}), f32[4096,128]{1,0:T(8,128)}) %all-gather.43.cloned.1.call-update) | async-done | bytes 2097168 | tf_op jit(solution)/shard_map/all_gather | solution.py:10
  643.5 1.7 reduce.14
  646.0 40.9 %all-gather.49.cloned.1.call-done = f32[16,256,128]{2,1,0:T(8,128)} async-done(((f32[1,256,128]{2,1,0:T(8,128)}), f32[16,256,128]{2,1,0:T(8,128)}) %all-gather.49.cloned.1.call-update) | async-done | bytes 2097168 | tf_op jit(solution)/shard_map/all_gather | solution.py:10
  686.9 1.7 reduce.15
  690.6 84.8 %all-gather.55.cloned.1.call-done = f32[8192,128]{1,0:T(8,128)} async-done(((f32[256,128]{1,0:T(8,128)}), f32[8192,128]{1,0:T(8,128)}) %all-gather.55.cloned.1.call-update) | async-done | bytes 4194320 | tf_op jit(solution)/shard_map/all_gather | solution.py:10
  775.4 2.4 reduce_sum.164
  777.8 85.4 %all-gather.61.cloned.1.call-done = f32[8192,128]{1,0:T(8,128)} async-done(((f32[256,128]{1,0:T(8,128)}), f32[8192,128]{1,0:T(8,128)}) %all-gather.61.cloned.1.call-update) | async-done | bytes 4194320 | tf_op jit(solution)/shard_map/all_gather | solution.py:10
  863.2 2.4 reduce_sum.167
  865.6 85.3 %all-gather.51.cloned.1.call-done = f32[8192,128]{1,0:T(8,128)} async-done(((f32[256,128]{1,0:T(8,128)}), f32[8192,128]{1,0:T(8,128)}) %all-gather.51.cloned.1.call-update) | async-done | bytes 4194320 | tf_op jit(solution)/shard_map/all_gather | solution.py:10
  950.9 2.4 reduce_sum.162
  953.7 85.0 %all-gather.53.cloned.1.call-done = f32[8192,128]{1,0:T(8,128)} async-done(((f32[256,128]{1,0:T(8,128)}), f32[8192,128]{1,0:T(8,128)}) %all-gather.53.cloned.1.call-update) | async-done | bytes 4194320 | tf_op jit(solution)/shard_map/all_gather | solution.py:10
  1038.7 2.4 reduce_sum.163
  1043.1 83.3 %all-gather.57.cloned.1.call-done = f32[8192,128]{1,0:T(8,128)} async-done(((f32[256,128]{1,0:T(8,128)}), f32[8192,128]{1,0:T(8,128)}) %all-gather.57.cloned.1.call-update) | async-done | bytes 4194320 | tf_op jit(solution)/shard_map/all_gather | solution.py:10
  1126.3 2.4 reduce_sum.165
  1128.7 85.3 %all-gather.59.cloned.1.call-done = f32[8192,128]{1,0:T(8,128)} async-done(((f32[256,128]{1,0:T(8,128)}), f32[8192,128]{1,0:T(8,128)}) %all-gather.59.cloned.1.call-update) | async-done | bytes 4194320 | tf_op jit(solution)/shard_map/all_gather | solution.py:10
  1214.0 2.4 reduce_sum.166
  1216.4 85.3 %all-gather.65.cloned.1.call-done = f32[8192,128]{1,0:T(8,128)} async-done(((f32[256,128]{1,0:T(8,128)}), f32[8192,128]{1,0:T(8,128)}) %all-gather.65.cloned.1.call-update) | async-done | bytes 4194320 | tf_op jit(solution)/shard_map/all_gather | solution.py:10
  1301.7 2.4 reduce_sum.169
  1304.9 84.5 %all-gather.63.cloned.1.call-done = f32[8192,128]{1,0:T(8,128)} async-done(((f32[256,128]{1,0:T(8,128)}), f32[8192,128]{1,0:T(8,128)}) %all-gather.63.cloned.1.call-update) | async-done | bytes 4194320 | tf_op jit(solution)/shard_map/all_gather | solution.py:10
  1389.4 2.4 reduce_sum.168
  (117 shorter events, 33.1 us)
Async XLA Ops:
  6.5 42.5 %copy-start.1 = (bf16[1,2,256,128]{3,2,1,0:T(8,128)(2,1)S(1)}, bf16[1,2,256,128]{3,2,1,0:T(8,128)(2,1)}, u32[]{:S(2)}) copy-start(bf16[1,2,256,128]{3,2,1,0:T(8,128)(2,1)} %param.9) | copy-start | bytes 393220
  6.5 145.6 %all-gather.37.cloned.1.call-start = ((), (), s32[]{:S(2)}) async-start(), calls=%async_computation.2 | async-start | bytes 8650752 | tf_op jit(solution)/shard_map/all_gather | solution.py:10
  45.3 151.2 %all-gather.33.cloned.1.call-start = ((), (), s32[]{:S(2)}) async-start(), calls=%async_computation | async-start | bytes 2228224 | tf_op jit(solution)/shard_map/all_gather | solution.py:10
  48.5 191.2 %all-gather.39.cloned.1.call-start = ((), (), s32[]{:S(2)}) async-start(), calls=%async_computation.3 | async-start | bytes 2228224 | tf_op jit(solution)/shard_map/all_gather | solution.py:10
  181.3 199.0 %all-gather.41.cloned.1.call-start = ((), (), s32[]{:S(2)}) async-start(), calls=%async_computation.4 | async-start | bytes 8650752 | tf_op jit(solution)/shard_map/all_gather | solution.py:10
  280.0 189.8 %all-gather.47.cloned.1.call-start = ((), (), s32[]{:S(2)}) async-start(), calls=%async_computation.7 | async-start | bytes 4325376 | tf_op jit(solution)/shard_map/all_gather | solution.py:10
  280.8 276.6 %all-gather.45.cloned.1.call-start = ((), (), s32[]{:S(2)}) async-start(), calls=%async_computation.6 | async-start | bytes 4325376 | tf_op jit(solution)/shard_map/all_gather | solution.py:10
  281.6 318.5 %all-gather.35.cloned.1.call-start = ((), (), s32[]{:S(2)}) async-start(), calls=%async_computation.1 | async-start | bytes 2228224 | tf_op jit(solution)/shard_map/all_gather | solution.py:10
  282.3 361.2 %all-gather.43.cloned.1.call-start = ((), (), s32[]{:S(2)}) async-start(), calls=%async_computation.5 | async-start | bytes 2228224 | tf_op jit(solution)/shard_map/all_gather | solution.py:10
  409.6 277.4 %all-gather.49.cloned.1.call-start = ((), (), s32[]{:S(2)}) async-start(), calls=%async_computation.8 | async-start | bytes 2228224 | tf_op jit(solution)/shard_map/all_gather | solution.py:10
  562.1 213.3 %all-gather.55.cloned.1.call-start = ((), (), s32[]{:S(2)}) async-start(), calls=%async_computation.11 | async-start | bytes 4325376 | tf_op jit(solution)/shard_map/all_gather | solution.py:10
  602.5 260.7 %all-gather.61.cloned.1.call-start = ((), (), s32[]{:S(2)}) async-start(), calls=%async_computation.14 | async-start | bytes 4325376 | tf_op jit(solution)/shard_map/all_gather | solution.py:10
  603.2 347.6 %all-gather.51.cloned.1.call-start = ((), (), s32[]{:S(2)}) async-start(), calls=%async_computation.9 | async-start | bytes 4325376 | tf_op jit(solution)/shard_map/all_gather | solution.py:10
  603.8 434.9 %all-gather.53.cloned.1.call-start = ((), (), s32[]{:S(2)}) async-start(), calls=%async_computation.10 | async-start | bytes 4325376 | tf_op jit(solution)/shard_map/all_gather | solution.py:10
  604.6 521.8 %all-gather.57.cloned.1.call-start = ((), (), s32[]{:S(2)}) async-start(), calls=%async_computation.12 | async-start | bytes 4325376 | tf_op jit(solution)/shard_map/all_gather | solution.py:10
  645.9 568.1 %all-gather.59.cloned.1.call-start = ((), (), s32[]{:S(2)}) async-start(), calls=%async_computation.13 | async-start | bytes 4325376 | tf_op jit(solution)/shard_map/all_gather | solution.py:10
  689.4 612.3 %all-gather.65.cloned.1.call-start = ((), (), s32[]{:S(2)}) async-start(), calls=%async_computation.16 | async-start | bytes 4325376 | tf_op jit(solution)/shard_map/all_gather | solution.py:10
  690.0 699.4 %all-gather.63.cloned.1.call-start = ((), (), s32[]{:S(2)}) async-start(), calls=%async_computation.15 | async-start | bytes 4325376 | tf_op jit(solution)/shard_map/all_gather | solution.py:10
  1304.5 88.7 %copy-start = (bf16[1,2,256,128]{3,2,1,0:T(8,128)(2,1)S(1)}, bf16[1,2,256,128]{3,2,1,0:T(8,128)(2,1)}, u32[]{:S(2)}) copy-start(bf16[1,2,256,128]{3,2,1,0:T(8,128)(2,1)} %param.8) | copy-start | bytes 393220
Sparse Core Ops, SparseCore 0:
  45.4 106.6 all-gather.36
  154.2 42.2 all-gather.32
  198.7 41.0 all-gather.38
  280.1 100.1 all-gather.40
  383.3 86.3 all-gather.46
  472.8 84.6 all-gather.44
  559.5 40.4 all-gather.34
  602.2 41.2 all-gather.42
  645.6 41.2 all-gather.48
  689.9 85.3 all-gather.54
  778.6 84.6 all-gather.60
  866.2 84.6 all-gather.50
  954.0 84.5 all-gather.52
  1041.7 84.5 all-gather.56
  1129.4 84.6 all-gather.58
  1217.0 84.6 all-gather.64
  1304.7 84.6 all-gather.62
